TPU v7x, 32 devices: a whole 2x2x4 slice. The times are simulated.
32 devices in a mesh: rec: 4 (over z), tm: 8 (over y, x, core).
Axes of the slice: x: 2, y: 2, z: 4, core: 2. Of those that a mesh axis runs over, the one named last changes fastest.
Arguments:
- frames: bfloat16 [8192, 1280], P(('rec', 'tm')), parts along dimension 0, may hold values from -50 to 50
- w_query: bfloat16 [1280, 1280], replicated, may hold values from -1 to 1
- w_kv: bfloat16 [1280, 2560], replicated, may hold values from -1 to 1
- w_out: bfloat16 [1280, 1280], replicated, may hold values from -0.15625 to 0.15625
- norm_gain: float32 [1280], replicated, may hold values from 0.5 to 1.5
- rand_owner: int32 [64, 3], P(('rec', 'tm')), parts along dimension 0, may hold values from 0 to 7, all different within a row; in each aligned block of 2 rows (0 to 1, 2 to 3, ...) at most 2 rows name the same one
- rand_slot: int32 [64, 3], P(('rec', 'tm')), parts along dimension 0, may hold values from 0 to 1
- global_pos: int32 [512], P('rec'), parts along dimension 0, may hold values from 0 to 2047
- length: int32 [4], P('rec'), parts along dimension 0, may hold values from 8 to 16
Outputs:
- pooled_out: bfloat16 [2048, 1280], P(('rec', 'tm')), parts along dimension 0
There are 4 independent parts, one for each index of `rec`. A program takes and returns all parts, laid end to end along the dimension named above; an argument that names none is the same for every part. Nothing has to cross between parts.
Inputs may be any that keep to these rules, and one draw needn't show every extreme that they name: `rand_owner`: the 3 owners of one query block differ; over the query blocks of one time shard no owner is named more than 2 times, a bound that some block reaches.
All inputs are finite; a program needn't handle non-finite values.
Results may differ from a plain program's by a relative error of at most 0.012.
The roundings to bfloat16 on the way count: a program that leaves them out, or rounds other values in their place, can miss the bound.
Values may be sent and summed in bfloat16 or wider, within the bound.
A program may use at most 128 MiB of HBM per device.

v0:
```python
import math

import jax
import jax.numpy as jnp
from jax import lax
from jax.sharding import PartitionSpec as P

HEADS = 20
BLOCK = 128
POOL = 4


def with_halo(value, sides, width):
    for axis, dim in sides:
        size, length = (lax.axis_size(axis), value.shape[dim])
        up = [(i, (i + 1) % size) for i in range(size - 1)]
        down = [(j, i) for i, j in up]
        last = lax.slice_in_dim(value, length - width, length, axis=dim)
        leading = lax.slice_in_dim(value, 0, width, axis=dim)
        before = lax.ppermute(last, axis, up)
        after = lax.ppermute(leading, axis, down)
        value = jnp.concatenate([before, value, after], axis=dim)
    return value


def attend(query_rows, key_rows, key_live, global_keys, global_live, head_count):
    group_size, block_rows, model_width = query_rows.shape
    head_size = model_width // head_count
    score_scale = head_size ** (-0.5)
    query_h = query_rows.reshape(group_size, block_rows, head_count, head_size)
    key_h = key_rows[..., :model_width].reshape(group_size, -1, head_count, head_size)
    value_h = key_rows[..., model_width:].reshape(group_size, -1, head_count, head_size)
    global_key_h = global_keys[:, :model_width].reshape(-1, head_count, head_size)
    global_value_h = global_keys[:, model_width:].reshape(-1, head_count, head_size)
    near_scores = (
        jnp.einsum("bihd,bjhd->bhij", query_h, key_h, preferred_element_type=jnp.float32)
        * score_scale
    )
    far_scores = (
        jnp.einsum("bihd,jhd->bhij", query_h, global_key_h, preferred_element_type=jnp.float32)
        * score_scale
    )
    near_scores = jnp.where(key_live[:, None, None, :], near_scores, -1e30)
    far_scores = jnp.where(global_live[None, None, None, :], far_scores, -1e30)
    row_max = jnp.maximum(jnp.max(near_scores, axis=-1), jnp.max(far_scores, axis=-1))[..., None]
    near_exp = jnp.exp(near_scores - row_max)
    far_exp = jnp.exp(far_scores - row_max)
    row_total = jnp.sum(near_exp, axis=-1, keepdims=True) + jnp.sum(far_exp, axis=-1, keepdims=True)
    near_weight = (near_exp / row_total).astype(jnp.bfloat16)
    far_weight = (far_exp / row_total).astype(jnp.bfloat16)
    context = jnp.einsum(
        "bhij,bjhd->bihd", near_weight, value_h, preferred_element_type=jnp.float32
    )
    context = context + jnp.einsum(
        "bhij,jhd->bihd", far_weight, global_value_h, preferred_element_type=jnp.float32
    )
    return context.reshape(group_size, block_rows, model_width).astype(jnp.bfloat16)


def body(frames, w_query, w_kv, w_out, norm_gain, rand_owner, rand_slot, global_pos, length):
    shards = lax.axis_size("tm")
    rank_here = lax.axis_index("tm")
    local_rows, model_width = frames.shape
    qblocks = local_rows // BLOCK
    pick_count = rand_owner.shape[1]
    first_block = rank_here * qblocks
    live_blocks = length[0]
    query_rows = jnp.dot(frames, w_query, preferred_element_type=jnp.float32).astype(jnp.bfloat16)
    keyval = jnp.dot(frames, w_kv, preferred_element_type=jnp.float32).astype(jnp.bfloat16)

    def project(rows):
        return jnp.dot(rows, w_kv, preferred_element_type=jnp.float32).astype(jnp.bfloat16)

    payload_width = frames.shape[1]
    padded = with_halo(frames, (("tm", 0),), BLOCK)
    lower_rim = project(padded[:BLOCK])
    upper_rim = project(padded[BLOCK + local_rows :])
    extended = jnp.concatenate([lower_rim, keyval, upper_rim], axis=0).reshape(
        qblocks + 2, BLOCK, 2 * model_width
    )
    window_rows = jnp.stack([extended[offset : offset + qblocks] for offset in range(3)], axis=1)
    window_rows = window_rows.reshape(qblocks, 3 * BLOCK, 2 * model_width)
    local_index = global_pos - first_block * BLOCK
    onehot = (local_index[:, None] == jnp.arange(local_rows, dtype=jnp.int32)[None, :]).astype(
        jnp.bfloat16
    )
    picked = jnp.dot(onehot, frames, preferred_element_type=jnp.float32)
    summed = lax.psum(picked.astype(jnp.bfloat16), "tm")
    global_keys = project(summed)
    global_live = global_pos < live_blocks * BLOCK
    owners = rand_owner.reshape(-1)
    slot_ids = rand_slot.reshape(-1)
    request_count = owners.shape[0]
    capacity = min(qblocks, (pick_count * qblocks + shards - 1) // shards + 1)
    request_index = jnp.arange(request_count, dtype=jnp.int32)
    same_owner = (owners[:, None] == owners[None, :]) & (
        request_index[None, :] < request_index[:, None]
    )
    owner_rank = jnp.sum(same_owner.astype(jnp.int32), axis=1)
    position = owners * capacity + owner_rank
    slot_index = jnp.arange(shards * capacity, dtype=jnp.int32)
    request_table = (
        jnp.sum(
            jnp.where(position[None, :] == slot_index[:, None], slot_ids[None, :] + 1, 0), axis=1
        )
        - 1
    )
    request_table = request_table.reshape(shards, capacity)
    asked_slots = lax.all_to_all(request_table, "tm", split_axis=0, concat_axis=0, tiled=True)
    chosen = jnp.clip(asked_slots.reshape(-1), 0, qblocks - 1)
    reply_blocks = jnp.take(frames.reshape(qblocks, BLOCK, payload_width), chosen, axis=0)
    reply_blocks = reply_blocks.reshape(shards, capacity, BLOCK, payload_width)
    answered = lax.all_to_all(reply_blocks, "tm", split_axis=0, concat_axis=0, tiled=True)
    fetched = jnp.take(answered.reshape(shards * capacity, BLOCK, payload_width), position, axis=0)
    random_rows = project(fetched.reshape(-1, payload_width)).reshape(
        qblocks, pick_count * BLOCK, 2 * model_width
    )
    key_rows = jnp.concatenate([window_rows, random_rows], axis=1)
    window_ids = (
        first_block
        + jnp.arange(qblocks, dtype=jnp.int32)[:, None]
        - 1
        + jnp.arange(3, dtype=jnp.int32)[None, :]
    )
    block_ids = jnp.concatenate([window_ids, rand_owner * qblocks + rand_slot], axis=1)
    key_live = jnp.repeat((block_ids >= 0) & (block_ids < live_blocks), BLOCK, axis=1)
    group_size = math.gcd(qblocks, max(1, 512 // BLOCK))
    group_count = qblocks // group_size

    def one_group(inputs):
        return attend(inputs[0], inputs[1], inputs[2], global_keys, global_live, HEADS)

    context = lax.map(
        one_group,
        (
            query_rows.reshape(group_count, group_size, BLOCK, model_width),
            key_rows.reshape(group_count, group_size, -1, 2 * model_width),
            key_live.reshape(group_count, group_size, -1),
        ),
    )
    context = context.reshape(local_rows, model_width)
    projected = jnp.dot(context, w_out, preferred_element_type=jnp.float32)
    pooled = jnp.mean(projected.reshape(local_rows // POOL, POOL, model_width), axis=1)
    feature_mean = jnp.mean(pooled, axis=1, keepdims=True)
    centered = pooled - feature_mean
    feature_var = jnp.mean(centered * centered, axis=1, keepdims=True)
    normed = centered * lax.rsqrt(feature_var + 1e-05) * norm_gain
    row_block = first_block + jnp.arange(local_rows // POOL, dtype=jnp.int32) * POOL // BLOCK
    return jnp.where((row_block < live_blocks)[:, None], normed, 0.0).astype(jnp.bfloat16)


def solution(mesh):
    placed = (
        P(("rec", "tm"), None),
        P(),
        P(),
        P(),
        P(),
        P(("rec", "tm"), None),
        P(("rec", "tm"), None),
        P("rec"),
        P("rec"),
    )
    return jax.shard_map(
        body, mesh=mesh, in_specs=placed, out_specs=P(("rec", "tm"), None), check_vma=False
    )
```

profile of v0, /device:TPU:0, one launch (start us, length us, event | category | flops | bytes accessed | tf_op | source)
XLA Modules:
  0.0 184.8 jit_solution(2662639635249441006)
XLA Ops:
  6.5 0.9 reshape.226
  7.5 0.8 fusion.26
  8.3 0.1 add.151
  8.4 0.2 convert_reduce_fusion
  8.6 0.1 select_reduce_fusion
  8.7 0.7 sub.52
  9.3 5.2 %all-to-all-start = ((s32[8,1,2]{2,1,0:T(1,128)}), s32[8,1,2]{2,1,0:T(1,128)S(1)}, u32[]{:S(2)}, u32[]{:S(2)}) async-start(s32[8,1,2]{2,1,0:T(1,128)} %bitcast.9), calls=%async_computation | async-start | bytes 8192 | tf_op jit(solution)/shard_map/all_to_all | solution.py:109
  14.6 2.0 %fusion.29 = (bf16[128,1280]{1,0:T(8,128)(2,1)}, bf16[128,1280]{1,0:T(8,128)(2,1)}) fusion(bf16[256,1280]{1,0:T(8,128)(2,1)} %param.9), kind=kLoop, calls=%fused_computation.91 | loop fusion | bytes 1310720 | tf_op jit(solution)/shard_map/slice | solution.py:18
  16.6 3.1 %collective-permute-start = (bf16[128,1280]{1,0:T(8,128)(2,1)}, bf16[128,1280]{1,0:T(8,128)(2,1)}, u32[]{:S(2)}, u32[]{:S(2)}) collective-permute-start(bf16[128,1280]{1,0:T(8,128)(2,1)} %get-tuple-element.34), channel_id=1, source_target_pairs={{0,1},{1,2},{2,3},{3,4},{4,5},{5,6},{6,7},{8,9},{9,10},{10,11},{11... | collective-permute-start | bytes 983048 | tf_op jit(solution)/shard_map/ppermute | solution.py:20
  19.7 1.3 collective-permute-start.1
  21.0 0.7 broadcast_subtract_fusion
  21.6 2.1 %convolution_convert_fusion.6 = bf16[128,1280]{1,0:T(8,128)(2,1)} fusion(bf16[256,1280]{1,0:T(8,128)(2,1)} %param.9, s32[128]{0:T(128)S(1)} %broadcast_subtract_fusion), kind=kOutput, calls=%fused_computation.27 | convolution fusion | flops 84082688 | bytes 983552 | tf_op jit(solution)/shard_map/dot_general | solution.py:87
  23.8 0.1 mul.74
  24.8 0.1 copy.82
  24.9 0.1 copy.83
  25.0 4.3 %gather_fusion = bf16[16,128,1280]{2,1,0:T(8,128)(2,1)} fusion(bf16[2,128,1280]{2,1,0:T(8,128)(2,1)} %bitcast.93, s32[1024]{0:T(1024)S(1)} %pad_clamp_fusion.1), kind=kCustom, calls=%fused_computation | custom fusion | bytes 10485824 | tf_op jit(solution)/shard_map/jit(_take)/gather | solution.py:111
  29.3 5.4 %broadcast_select_fusion = bf16[8,2,128,1280]{3,2,1,0:T(8,128)(2,1)} fusion(bf16[8,2,128,1280]{3,2,1,0:T(8,128)(2,1)} %bitcast.94, pred[8,2]{1,0:T(8,128)(4,1)S(1)} %copy.83), kind=kLoop, calls=%fused_computation.10 | loop fusion | flops 2621440 | bytes 10485776 | tf_op jit(solution)/shard_map/jit(_take)/select_n | solution.py:111
  34.7 5.5 %all-to-all-start.1 = ((bf16[8,2,128,1280]{3,2,1,0:T(8,128)(2,1)}), bf16[8,2,128,1280]{3,2,1,0:T(8,128)(2,1)}, u32[]{:S(2)}, u32[]{:S(2)}) async-start(bf16[8,2,128,1280]{3,2,1,0:T(8,128)(2,1)} %broadcast_select_fusion), calls=%async_computation.1 | async-start | bytes 10485760 | tf_op jit(solution)/shard_map/all_to_all | solution.py:113
  40.3 3.0 %convolution_convert_fusion.5 = bf16[256,1280]{1,0:T(8,128)(2,1)} fusion(bf16[256,1280]{1,0:T(8,128)(2,1)} %param.9, bf16[1280,1280]{1,0:T(8,128)(2,1)S(1)} %copy-done), kind=kOutput, calls=%fused_computation.26 | convolution fusion | flops 839188480 | bytes 4587520 | tf_op jit(solution)/shard_map/dot_general | solution.py:68
  43.3 5.9 %convolution_convert_fusion.1 = bf16[256,2560]{1,0:T(8,128)(2,1)} fusion(bf16[256,1280]{1,0:T(8,128)(2,1)S(1)} %copy-done.2, bf16[1280,2560]{1,0:T(8,128)(2,1)} %param.11), kind=kOutput, calls=%fused_computation.15 | convolution fusion | flops 1678376960 | bytes 8519680 | tf_op jit(solution)/shard_map/dot_general | solution.py:69
  49.2 0.2 copy.85
  49.4 0.2 reshape.231
  49.6 53.7 %all-reduce.2.cloned.1.call-done = bf16[128,1280]{1,0:T(8,128)(2,1)} async-done(((bf16[128,1280]{1,0:T(8,128)(2,1)}), bf16[128,1280]{1,0:T(8,128)(2,1)}) %all-reduce.2.cloned.1.call-update) | async-done | bytes 327696 | tf_op jit(solution)/shard_map/psum | solution.py:88
  103.3 4.0 %convolution_convert_fusion.2 = bf16[128,2560]{1,0:T(8,128)(2,1)S(1)} fusion(bf16[128,1280]{1,0:T(8,128)(2,1)} %all-reduce.2.cloned.1.call-done, bf16[1280,2560]{1,0:T(8,128)(2,1)} %param.11), kind=kOutput, calls=%fused_computation.16 | convolution fusion | flops 839188480 | bytes 7536640 | tf_op jit(solution)/shard_map/dot_general | solution.py:72
  107.4 0.9 copy.88
  108.3 0.9 copy.93
  109.2 1.8 bitcast_reduce_fusion
  111.0 4.1 %convolution_convert_fusion.4 = bf16[128,2560]{1,0:T(8,128)(2,1)S(1)} fusion(bf16[128,1280]{1,0:T(8,128)(2,1)} %collective-permute-done, bf16[1280,2560]{1,0:T(8,128)(2,1)} %param.11), kind=kOutput, calls=%fused_computation.18 | convolution fusion | flops 839188480 | bytes 7536640 | tf_op jit(solution)/shard_map/dot_general | solution.py:72
  115.2 2.1 %convolution_convert_fusion.3 = bf16[128,2560]{1,0:T(8,128)(2,1)S(1)} fusion(bf16[128,1280]{1,0:T(8,128)(2,1)} %collective-permute-done.1, bf16[1280,2560]{1,0:T(8,128)(2,1)S(1)} %bitcast.92), kind=kOutput, calls=%fused_computation.17 | convolution fusion | flops 839188480 | bytes 7536640 | tf_op jit(solution)/shard_map/dot_general | solution.py:72
  117.3 0.2 pad_maximum_fusion.3
  117.5 2.2 %pad_maximum_fusion.1 = bf16[2,3,128,2560]{3,2,1,0:T(8,128)(2,1)} fusion(bf16[2,1,128,2560]{3,2,1,0:T(8,128)(2,1)S(1)} %bitcast.99, bf16[2,1,128,2560]{3,2,1,0:T(8,128)(2,1)S(1)} %bitcast.97, bf16[2,1,128,2560]{3,2,1,0:T(8,128)(2,1)S(1)} %bitcast.98), kind=kLoop, calls=%fused_computation.14 | loop fusion | flops 3932160 | bytes 7864320 | tf_op jit(solution)/shard_map/stack | solution.py:81
  119.8 4.5 %gather_fusion.1 = bf16[6,128,1280]{2,1,0:T(8,128)(2,1)} fusion(bf16[16,128,1280]{2,1,0:T(8,128)(2,1)} %bitcast.14, s32[1024]{0:T(1024)S(1)} %pad_clamp_fusion), kind=kCustom, calls=%fused_computation.1 | custom fusion | bytes 3932184 | tf_op jit(solution)/shard_map/jit(_take)/gather | solution.py:114
  124.3 1.8 bitcast_select_fusion
  126.1 8.5 %convolution_convert_fusion = bf16[768,2560]{1,0:T(8,128)(2,1)S(1)} fusion(bf16[768,1280]{1,0:T(8,128)(2,1)S(1)} %bitcast_select_fusion, bf16[1280,2560]{1,0:T(8,128)(2,1)} %param.11), kind=kOutput, calls=%fused_computation.11 | convolution fusion | flops 5035130880 | bytes 12451840 | tf_op jit(solution)/shard_map/dot_general | solution.py:72
  134.6 3.4 %pad_maximum_fusion = (bf16[2,768,1280]{2,1,0:T(8,128)(2,1)}, bf16[2,768,1280]{2,1,0:T(8,128)(2,1)}) fusion(bf16[2,384,2560]{2,1,0:T(8,128)(2,1)S(1)} %bitcast.101, bf16[2,384,2560]{2,1,0:T(8,128)(2,1)S(1)} %bitcast.96), kind=kLoop, calls=%fused_computation.13 | loop fusion | flops 15728640 | bytes 15728640 | tf_op jit(solution)/shard_map/concatenate | solution.py:118
  138.0 6.3 %copy.84 = bf16[2,768,1280]{1,2,0:T(8,128)(2,1)} copy(bf16[2,768,1280]{2,1,0:T(8,128)(2,1)} %get-tuple-element.20) | data formatting | bytes 7864320 | tf_op jit(solution)/shard_map/while/body/eval_jaxpr/slice | solution.py:32
  144.3 6.3 %copy.86 = bf16[2,768,1280]{1,2,0:T(8,128)(2,1)} copy(bf16[2,768,1280]{2,1,0:T(8,128)(2,1)} %get-tuple-element.19) | data formatting | bytes 7864320 | tf_op jit(solution)/shard_map/while/body/eval_jaxpr/slice | solution.py:31
  150.6 4.3 %fusion = (f32[2,20,128]{2,1,0:T(8,128)S(1)}, f32[2,20,128,768]{3,2,1,0:T(8,128)S(1)}) fusion(pred[2,768]{1,0:T(4,128)(4,1)S(1)} %bitcast.104, bf16[2,768,20,64]{1,3,2,0:T(8,128)(2,1)} %bitcast.95, bf16[2,128,20,64]{1,0,3,2:T(2,128)(2,1)S(1)} %reshape.231), kind=kOutput, calls=%fused_computation.5 | convolution fusion | flops 515107840 | bytes 20338176 | tf_op jit(solution)/shard_map/while/body/eval_jaxpr/bihd,bjhd->bhij/dot_general | solution.py:36
  154.9 4.0 %fusion.1 = f32[2,20,128]{2,1,0:T(8,128)S(1)} fusion(f32[2,20,128,768]{3,2,1,0:T(8,128)S(1)} %get-tuple-element.42, f32[2,20,128]{2,1,0:T(8,128)S(1)} %copy_maximum_fusion, pred[2,768]{1,0:T(4,128)(4,1)S(1)} %bitcast.105), kind=kLoop, calls=%fused_computation.6 | loop fusion | flops 15723520 | bytes 15771136 | tf_op jit(solution)/shard_map/while/body/eval_jaxpr/reduce_sum | solution.py:48
  158.9 0.7 fusion.7
  159.7 6.5 %fusion.8 = f32[2,128,20,64]{1,3,2,0:T(8,128)} fusion(bf16[2,768,20,64]{1,3,2,0:T(8,128)(2,1)S(1)} %bitcast.100, f32[2,20,128,768]{3,2,1,0:T(8,128)S(1)} %get-tuple-element.42, f32[2,20,128]{2,1,0:T(8,128)S(1)} %copy_add_fusion, f32[2,20,128]{2,1,0:T(8,128)S(1)} %copy_maximum_fusion, pred[2,768]{1,0:T(4,128)(4,1)S(1)} %bitcast.106), kind=kOutput, calls=%fused_computation.30 | convolution fusion | flops 522977280 | bytes 21014016 | tf_op jit(solution)/shard_map/while/body/eval_jaxpr/bhij,bjhd->bihd/dot_general | solution.py:51
  166.3 2.2 %fusion.10 = bf16[2,128,20,64]{1,3,2,0:T(8,128)(2,1)S(1)} fusion(f32[2,128,20,64]{1,3,2,0:T(8,128)} %fusion.8, bf16[128,20,64,1]{0,2,1,3:T(8,128)(2,1)S(1)} %bitcast.103, f32[20,128,2,128]{3,1,2,0:T(8,128)S(1)} %get-tuple-element.44, f32[2,20,128]{2,0,1:T(2,128)S(1)} %copy.94, f32[2,20,128]{2,0,1:T(2,128)S(1)} %copy.91, ...), kind=kOutput, calls=%fused_computation.33 | convolution fusion | flops 87818240 | bytes 4956288 | tf_op jit(solution)/shard_map/while/body/eval_jaxpr/bhij,jhd->bihd/dot_general | solution.py:54
  168.5 1.7 copy.96
  170.2 3.4 %convert_element_type.56 = bf16[64,4,1280]{2,1,0:T(4,128)(2,1)} reshape(bf16[2,128,20,64]{3,2,1,0:T(8,128)(2,1)} %copy.96) | data formatting | bytes 1310720 | tf_op jit(solution)/shard_map/while/body/eval_jaxpr/convert_element_type | solution.py:57
  173.6 3.2 %fusion.12 = f32[64,1280]{1,0:T(8,128)S(1)} fusion(bf16[1280,1280]{1,0:T(8,128)(2,1)} %param.12, bf16[64,4,1280]{2,1,0:T(4,128)(2,1)} %convert_element_type.56), kind=kOutput, calls=%fused_computation.37 | convolution fusion | flops 839106560 | bytes 4259840 | tf_op jit(solution)/shard_map/dot_general | solution.py:142
  176.8 0.1 multiply_reduce_fusion.1
  176.9 0.2 multiply_reduce_fusion
  177.2 0.8 select_convert_fusion
  (54 shorter events, 0.6 us)
Async XLA Ops:
  6.5 33.8 %copy-start = (bf16[1280,1280]{1,0:T(8,128)(2,1)S(1)}, bf16[1280,1280]{1,0:T(8,128)(2,1)}, u32[]{:S(2)}) copy-start(bf16[1280,1280]{1,0:T(8,128)(2,1)} %param.10) | copy-start | bytes 9830404
  9.3 15.3 %all-to-all-start = ((s32[8,1,2]{2,1,0:T(1,128)}), s32[8,1,2]{2,1,0:T(1,128)S(1)}, u32[]{:S(2)}, u32[]{:S(2)}) async-start(s32[8,1,2]{2,1,0:T(1,128)} %bitcast.9), calls=%async_computation | async-start | bytes 8192 | tf_op jit(solution)/shard_map/all_to_all | solution.py:109
  14.5 88.8 %all-reduce.2.cloned.1.call-start = ((), (), s32[]{:S(2)}) async-start(), calls=%async_computation.2 | async-start | bytes 655360 | tf_op jit(solution)/shard_map/psum | solution.py:88
  16.6 94.5 %collective-permute-start = (bf16[128,1280]{1,0:T(8,128)(2,1)}, bf16[128,1280]{1,0:T(8,128)(2,1)}, u32[]{:S(2)}, u32[]{:S(2)}) collective-permute-start(bf16[128,1280]{1,0:T(8,128)(2,1)} %get-tuple-element.34), channel_id=1, source_target_pairs={{0,1},{1,2},{2,3},{3,4},{4,5},{5,6},{6,7},{8,9},{9,10},{10,11},{11... | collective-permute-start | bytes 983048 | tf_op jit(solution)/shard_map/ppermute | solution.py:20
  19.7 95.5 %collective-permute-start.1 = (bf16[128,1280]{1,0:T(8,128)(2,1)}, bf16[128,1280]{1,0:T(8,128)(2,1)}, u32[]{:S(2)}, u32[]{:S(2)}) collective-permute-start(bf16[128,1280]{1,0:T(8,128)(2,1)} %get-tuple-element.35), channel_id=1, source_target_pairs={{1,0},{2,1},{3,2},{4,3},{5,4},{6,5},{7,6},{9,8},{10,9},{11,10},{12... | collective-permute-start | bytes 983048 | tf_op jit(solution)/shard_map/ppermute | solution.py:21
  34.7 5.5 %copy-start.9 = (s32[128]{0:T(128)S(1)}, s32[128]{0:T(128)}, u32[]{:S(2)}) copy-start(s32[128]{0:T(128)} %param.16) | copy-start | bytes 1540
  34.7 85.1 %all-to-all-start.1 = ((bf16[8,2,128,1280]{3,2,1,0:T(8,128)(2,1)}), bf16[8,2,128,1280]{3,2,1,0:T(8,128)(2,1)}, u32[]{:S(2)}, u32[]{:S(2)}) async-start(bf16[8,2,128,1280]{3,2,1,0:T(8,128)(2,1)} %broadcast_select_fusion), calls=%async_computation.1 | async-start | bytes 10485760 | tf_op jit(solution)/shard_map/all_to_all | solution.py:113
  40.2 3.1 %copy-start.2 = (bf16[256,1280]{1,0:T(8,128)(2,1)S(1)}, bf16[256,1280]{1,0:T(8,128)(2,1)}, u32[]{:S(2)}) copy-start(bf16[256,1280]{1,0:T(8,128)(2,1)} %param.9) | copy-start | bytes 1966084
  43.3 5.9 %copy-start.6 = (bf16[256,1280]{1,0:T(8,128)(2,1)S(1)}, bf16[256,1280]{1,0:T(8,128)(2,1)}, u32[]{:S(2)}) copy-start(bf16[256,1280]{1,0:T(8,128)(2,1)} %convolution_convert_fusion.5) | copy-start | bytes 1966084
  109.2 6.0 %slice-start = ((s8[6553600]{0:T(1024)(128)(4,1)}), s8[4194304]{0:T(1024)(128)(4,1)S(1)}, s32[]{:S(2)}) async-start(s8[6553600]{0:T(1024)(128)(4,1)} %bitcast.91), calls=%async_computation.3 | async-start | bytes 8388608
  111.0 4.2 %slice-start.1 = ((s8[6553600]{0:T(1024)(128)(4,1)}), s8[2359296]{0:T(1024)(128)(4,1)S(1)}, s32[]{:S(2)}) async-start(s8[6553600]{0:T(1024)(128)(4,1)} %bitcast.91), calls=%async_computation.4 | async-start | bytes 4718592
  115.2 2.1 %copy-start.4 = (bf16[256,2560]{1,0:T(8,128)(2,1)S(1)}, bf16[256,2560]{1,0:T(8,128)(2,1)}, u32[]{:S(2)}) copy-start(bf16[256,2560]{1,0:T(8,128)(2,1)} %convolution_convert_fusion.1) | copy-start | bytes 3932164
  126.1 8.5 %copy-start.3 = (bf16[2,3,128,2560]{3,2,1,0:T(8,128)(2,1)S(1)}, bf16[2,3,128,2560]{3,2,1,0:T(8,128)(2,1)}, u32[]{:S(2)}) copy-start(bf16[2,3,128,2560]{3,2,1,0:T(8,128)(2,1)} %pad_maximum_fusion.1) | copy-start | bytes 11796484
  154.9 4.8 %copy-start.5 = (bf16[2,768,1280]{1,2,0:T(8,128)(2,1)S(1)}, bf16[2,768,1280]{1,2,0:T(8,128)(2,1)}, u32[]{:S(2)}) copy-start(bf16[2,768,1280]{1,2,0:T(8,128)(2,1)} %copy.84) | copy-start | bytes 11796484
  159.7 6.6 %copy-start.7 = (bf16[128,1280]{0,1:T(8,128)(2,1)S(1)}, bf16[128,1280]{0,1:T(8,128)(2,1)}, u32[]{:S(2)}) copy-start(bf16[128,1280]{0,1:T(8,128)(2,1)} %copy.93) | copy-start | bytes 983044
  170.2 7.8 %copy-start.1 = (bf16[1280,1280]{1,0:T(8,128)(2,1)S(1)}, bf16[1280,1280]{1,0:T(8,128)(2,1)}, u32[]{:S(2)}) copy-start(bf16[1280,1280]{1,0:T(8,128)(2,1)} %param.10) | copy-start | bytes 9830404
  173.6 3.5 %copy-start.8 = (f32[1280]{0:T(1024)S(1)}, f32[1280]{0:T(1024)}, u32[]{:S(2)}) copy-start(f32[1280]{0:T(1024)} %param.13) | copy-start | bytes 15364
Sparse Core Ops, SparseCore 0:
  23.9 79.4 all-reduce.1
where the time goes:
time: 186 us; the launch traced here: 185 us
  waiting for transfers between devices  53.8 us (29%)
  matrix products  47.7 us (26%)
  local copies, waits for them, and re-layouts  32.9 us (18%)
  other arithmetic  20.9 us (11%)
  starting transfers between devices  15.1 us (8%)
  between operations  14.4 us (8%)
    psum x1, waiting for transfers between devices, body(): summed = lax.psum(picked.astype(jnp.bfloat16), 'tm')  53.7 us
    dot_general x4, matrix products, project(): jnp.dot(rows, w_kv, preferred_element_type=jnp.float32).astype(jnp.bfloat16)  18.7 us
    dot_general x1, matrix products, attend(): jnp.einsum('bhij,bjhd->bihd', near_weight, value_h, preferred_element_typ...  6.55 us
    slice x1, local copies, waits for them, and re-layouts, attend(): key_rows[..., model_width:].reshape(group_size, -1, head_count, head_size)  6.28 us
    slice x1, local copies, waits for them, and re-layouts, attend(): key_rows[..., :model_width].reshape(group_size, -1, head_count, head_size)  6.28 us
    dot_general x1, matrix products, body(): jnp.dot(frames, w_kv, preferred_element_type=jnp.float32)  5.86 us
    all_to_all x1, starting transfers between devices, body(): lax.all_to_all(reply_blocks, 'tm', split_axis=0, concat_axis=0, tiled=True)  5.52 us
    select_n x2, other arithmetic, body(): jnp.take(frames.reshape(qblocks, BLOCK, payload_width), chosen, axis=0)  5.41 us
  transfers between devices with their start and end apart: 5, of which 1 were waited for; matrix products, arithmetic and copies ran while one was open for 22% of the time, Pallas kernels for 0%

commit v1 on v0

v1 whole, which is shorter than its diff:
```python
import functools

import jax
import jax.numpy as jnp
from jax import lax
from jax.experimental import pallas as pl
from jax.experimental.pallas import tpu as pltpu
from jax.sharding import PartitionSpec as P

HEADS = 20
BLOCK = 128
POOL = 4
TILE = 512
MESH = pl.DeviceIdType.MESH
F32 = jnp.float32
BF16 = jnp.bfloat16


def kernel(shards, frames, w_query, w_kv, w_out, gain, owner, slot, gpos, length, out,
           fall, kv, wq_v, wkv_v, wout_v, q_v, gacc, gkv, pctx, proj, lsem, ssem, rsem, psem):
    me = lax.axis_index("tm")
    width = wq_v.shape[0]
    picks = owner.shape[1]
    first = me * 2
    count = [0]
    sends = []

    def local(src, dst, index):
        copy = pltpu.make_async_copy(src, dst, lsem.at[index])
        copy.start()
        return copy

    def send(src, shard, part, target):
        copy = pltpu.make_async_remote_copy(
            src_ref=src, dst_ref=fall.at[shard, part], send_sem=ssem.at[count[0]],
            recv_sem=rsem.at[shard, part], device_id={"tm": target}, device_id_type=MESH)
        count[0] += 1
        copy.start()
        sends.append(copy)

    def arrived(shard, part):
        pltpu.make_async_copy(fall.at[shard, part], fall.at[shard, part],
                              rsem.at[shard, part]).wait()

    own = local(frames, fall.at[me], 0)
    got_q = local(w_query, wq_v, 1)
    got_kv = local(w_kv, wkv_v, 2)
    got_out = local(w_out, wout_v, 3)

    if shards == 8:
        side = me + 1 - 2 * (me % 2)
        near_x = me + 2 - 4 * ((me // 2) % 2)
        near_y = (me + 4) % 8
        partners = [side, near_x, near_y]
    else:
        partners = [(me + k) % shards for k in range(1, shards)]
    barrier = pltpu.get_barrier_semaphore()
    for target in partners:
        pl.semaphore_signal(barrier, inc=1, device_id={"tm": target}, device_id_type=MESH)
    pl.semaphore_wait(barrier, len(partners))
    if shards == 8:
        send(frames.at[0], me, 0, near_x)
        send(frames.at[1], me, 1, near_y)
        send(frames.at[1], me, 1, near_x)
        send(frames.at[0], me, 0, near_y)
        send(frames.at[0], me, 0, side)
        send(frames.at[1], me, 1, side)
    else:
        for target in partners:
            send(frames.at[0], me, 0, target)
            send(frames.at[1], me, 1, target)

    gacc[...] = jnp.zeros_like(gacc)
    pos_t = jnp.broadcast_to(gpos[...], (BLOCK, BLOCK)).T
    lane = lax.broadcasted_iota(jnp.int32, (BLOCK, BLOCK), 1)

    def onehot(block):
        return jnp.where(pos_t == block * BLOCK + lane, 1.0, 0.0).astype(BF16)

    def project(shard_a, part_a, shard_b, part_b):
        block_a, block_b = shard_a * 2 + part_a, shard_b * 2 + part_b
        hot = jnp.concatenate([onehot(block_a), onehot(block_b)], axis=1)

        def step(n, carry):
            cols = pl.ds(pl.multiple_of(n * TILE, TILE), TILE)
            rows = jnp.concatenate([fall[shard_a, part_a], fall[shard_b, part_b]], axis=0)
            made = jnp.dot(rows, wkv_v[:, cols], preferred_element_type=F32).astype(BF16)
            kv[block_a, :, cols] = made[:BLOCK]
            kv[block_b, :, cols] = made[BLOCK:]
            gacc[:, cols] += jnp.dot(hot, made, preferred_element_type=F32)
            return carry

        lax.fori_loop(0, 2 * width // TILE, step, 0)

    own.wait()
    got_q.wait()

    def query_step(n, carry):
        cols = pl.ds(pl.multiple_of(n * 256, 256), 256)
        rows = jnp.concatenate([fall[me, 0], fall[me, 1]], axis=0)
        made = jnp.dot(rows, wq_v[:, cols], preferred_element_type=F32).astype(BF16)
        q_v[:, cols] = (made.astype(F32) * 0.125).astype(BF16)
        return carry

    lax.fori_loop(0, width // 256, query_step, 0)
    got_kv.wait()
    project(me, 0, me, 1)
    if shards == 8:
        diag = near_x + near_y - me
        side_x, side_y = (v + 1 - 2 * (v % 2) for v in (near_x, near_y))
        side_d = diag + 1 - 2 * (diag % 2)
        arrived(side, 0)
        arrived(side, 1)
        project(side, 0, side, 1)
        arrived(near_x, 0)
        send(fall.at[near_x, 0], near_x, 0, near_y)
        send(fall.at[near_x, 0], near_x, 0, side)
        arrived(near_y, 1)
        send(fall.at[near_y, 1], near_y, 1, near_x)
        send(fall.at[near_y, 1], near_y, 1, side)
        project(near_x, 0, near_y, 1)
        arrived(side_x, 0)
        arrived(side_y, 1)
        project(side_x, 0, side_y, 1)
        arrived(near_x, 1)
        send(fall.at[near_x, 1], near_x, 1, side)
        arrived(near_y, 0)
        send(fall.at[near_y, 0], near_y, 0, side)
        project(near_x, 1, near_y, 0)
        arrived(side_x, 1)
        arrived(side_y, 0)
        project(side_x, 1, side_y, 0)
        arrived(diag, 0)
        send(fall.at[diag, 0], diag, 0, side)
        arrived(diag, 1)
        send(fall.at[diag, 1], diag, 1, side)
        project(diag, 0, diag, 1)
        arrived(side_d, 0)
        arrived(side_d, 1)
        project(side_d, 0, side_d, 1)
    else:
        for k in range(1, shards):
            source = (me + shards - k) % shards
            arrived(source, 0)
            arrived(source, 1)
            project(source, 0, source, 1)
    gkv[...] = gacc[...].astype(BF16)

    live = length[0]
    low = jnp.where(lane < 64, 1.0, 0.0).astype(BF16)
    high = jnp.where(lane < 64, 0.0, 1.0).astype(BF16)
    pool_row = lax.broadcasted_iota(jnp.int32, (BLOCK // POOL, BLOCK), 0)
    pool_col = lax.broadcasted_iota(jnp.int32, (BLOCK // POOL, BLOCK), 1)
    pool = jnp.where(pool_col // POOL == pool_row, 1.0 / POOL, 0.0).astype(BF16)
    far_bias = jnp.where(gpos[...] < live * BLOCK, 0.0, -1e30)
    blocks, biases = [], []
    for b in range(2):
        ids = [first + b - 1 + k for k in range(3)]
        ids += [owner[b, j] * 2 + slot[b, j] for j in range(picks)]
        blocks.append([jnp.clip(i, 0, 2 * shards - 1) for i in ids])
        row = [jnp.full((1, BLOCK), jnp.where((i >= 0) & (i < live), 0.0, -1e30), F32) for i in ids]
        biases.append(jnp.concatenate(row + [far_bias], axis=1))

    def pair_step(p, carry):
        kcols = pl.ds(pl.multiple_of(p * 128, 128), 128)
        vcols = pl.ds(pl.multiple_of(width + p * 128, 128), 128)
        for b in range(2):
            q = q_v[b * BLOCK:(b + 1) * BLOCK, kcols]
            qs = jnp.concatenate([q * low, q * high], axis=0)
            keys = jnp.concatenate([kv[i, :, kcols] for i in blocks[b]] + [gkv[:, kcols]], axis=0)
            vals = jnp.concatenate([kv[i, :, vcols] for i in blocks[b]] + [gkv[:, vcols]], axis=0)
            s = lax.dot_general(qs, keys, (((1,), (1,)), ((), ())), preferred_element_type=F32)
            s = s + biases[b]
            e = jnp.exp(s - jnp.max(s, axis=1, keepdims=True))
            total = jnp.sum(e, axis=1, keepdims=True)
            o = jnp.dot(e.astype(BF16), vals, preferred_element_type=F32) / total
            c = jnp.where(lane < 64, o[:BLOCK], o[BLOCK:]).astype(BF16)
            pctx[b * 32:(b + 1) * 32, kcols] = jnp.dot(pool, c, preferred_element_type=F32)
        return carry

    lax.fori_loop(0, width // 128, pair_step, 0)
    got_out.wait()
    rows = pctx.shape[0]
    upper = pctx[...].astype(BF16)
    lower = (pctx[...] - upper.astype(F32)).astype(BF16)
    both = jnp.concatenate([upper, lower], axis=0)
    for n in range(width // 256):
        made = jnp.dot(both, wout_v[:, n * 256:(n + 1) * 256], preferred_element_type=F32)
        proj[:, n * 256:(n + 1) * 256] = made[:rows] + made[rows:]
    pooled = proj[...]
    centered = pooled - jnp.mean(pooled, axis=1, keepdims=True)
    var = jnp.mean(centered * centered, axis=1, keepdims=True)
    normed = centered * lax.rsqrt(var + 1e-05) * gain[...]
    row_block = first + lax.broadcasted_iota(jnp.int32, (rows, width), 0) * POOL // BLOCK
    out[...] = jnp.where(row_block < live, normed, 0.0).astype(BF16)
    for copy in sends:
        copy.wait_send()


def body(shards, frames, w_query, w_kv, w_out, norm_gain, rand_owner, rand_slot, global_pos, length):
    local_rows, width = frames.shape
    assert local_rows == 2 * BLOCK and width == HEADS * 64 and global_pos.shape[0] == BLOCK
    hbm = pl.BlockSpec(memory_space=pl.ANY)
    vmem = pl.BlockSpec(memory_space=pltpu.VMEM)
    smem = pl.BlockSpec(memory_space=pltpu.SMEM)
    n_sends = 14 if shards == 8 else 2 * (shards - 1)
    return pl.pallas_call(
        functools.partial(kernel, shards),
        out_shape=jax.ShapeDtypeStruct((local_rows // POOL, width), BF16),
        in_specs=[hbm, hbm, hbm, hbm, vmem, smem, smem, vmem, smem],
        out_specs=vmem,
        scratch_shapes=[
            pltpu.VMEM((shards, 2, BLOCK, width), BF16),
            pltpu.VMEM((2 * shards, BLOCK, 2 * width), BF16),
            pltpu.VMEM((width, width), BF16),
            pltpu.VMEM((width, 2 * width), BF16),
            pltpu.VMEM((width, width), BF16),
            pltpu.VMEM((local_rows, width), BF16),
            pltpu.VMEM((BLOCK, 2 * width), F32),
            pltpu.VMEM((BLOCK, 2 * width), BF16),
            pltpu.VMEM((local_rows // POOL, width), F32),
            pltpu.VMEM((local_rows // POOL, width), F32),
            pltpu.SemaphoreType.DMA((4,)),
            pltpu.SemaphoreType.DMA((n_sends,)),
            pltpu.SemaphoreType.DMA((shards, 2)),
            pltpu.SemaphoreType.DMA((1,)),
        ],
        compiler_params=pltpu.CompilerParams(
            collective_id=0, has_side_effects=True, vmem_limit_bytes=60 * 1024 * 1024),
        cost_estimate=pl.CostEstimate(
            flops=20_000_000_000, bytes_accessed=20_000_000, transcendentals=5_000_000),
    )(frames.reshape(2, BLOCK, width), w_query, w_kv, w_out, norm_gain.reshape(1, width),
      rand_owner, rand_slot, global_pos.reshape(1, BLOCK), length)


def solution(mesh):
    placed = (
        P(("rec", "tm"), None), P(), P(), P(), P(),
        P(("rec", "tm"), None), P(("rec", "tm"), None), P("rec"), P("rec"),
    )
    return jax.shard_map(
        functools.partial(body, mesh.shape["tm"]), mesh=mesh, in_specs=placed,
        out_specs=P(("rec", "tm"), None), check_vma=False)
```

time: 186 us -> 54.7 us (0.29)
  waiting for transfers between devices: 53.8 us -> 0 us
  Pallas kernels: 0 us -> 50.8 us
  matrix products: 47.7 us -> 0 us
  local copies, waits for them, and re-layouts: 32.9 us -> 2.89 us
  other arithmetic: 20.9 us -> 0 us
  starting transfers between devices: 15.1 us -> 0 us
  between operations: 14.4 us -> 0.66 us
    psum x1 -> x0, waiting for transfers between devices: 53.7 us -> none  [body(): summed = lax.psum(picked.astype(jnp.bfloat16), 'tm')]
    pallas_call x0 -> x1, Pallas kernels: none -> 50.8 us  [body(): pl.pallas_call(functools.partial(kernel, shards), out_shape=jax.ShapeDtyp...]
    dot_general x12 -> x0, matrix products: 47.7 us -> none  [the longest x4 18.7 us: project(): jnp.dot(rows, w_kv, preferred_element_type=jnp.float32).astype(jnp.bfloat16)]
    slice x6 -> x0, local copies, waits for them, and re-layouts: 16.4 us -> none  [the longest x1 6.28 us: attend(): key_rows[..., model_width:].reshape(group_size, -1, head_count, head_size)]
    all_to_all x2 -> x0, starting transfers between devices: 10.7 us -> none  [the longest x1 5.52 us: body(): lax.all_to_all(reply_blocks, 'tm', split_axis=0, concat_axis=0, tiled=True)]
    gather x2 -> x0, local copies, waits for them, and re-layouts: 8.82 us -> none  [the longest x1 4.54 us: body(): jnp.take(answered.reshape(shards * capacity, BLOCK, payload_width), posit...]
    select_n x4 -> x0, other arithmetic: 7.2 us -> none  [the longest x2 5.41 us: body(): jnp.take(frames.reshape(qblocks, BLOCK, payload_width), chosen, axis=0)]
    reduce_sum x6 -> x0, other arithmetic: 5.36 us -> none  [the longest x1 4.04 us: attend(): jnp.sum(near_exp, axis=-1, keepdims=True)]
  transfers between devices with their start and end apart: 5 -> 0, of which waited for: 1 -> 0; matrix products, arithmetic and copies ran while one was open for 22% -> 0% of each run, Pallas kernels for 0% -> 0%
where the time goes in v1:
time: 54.7 us; the launch traced here: 54.4 us
  Pallas kernels  50.8 us (93%)
  local copies, waits for them, and re-layouts  2.89 us (5%)
  between operations  0.66 us (1%)
    pallas_call x1, Pallas kernels, body(): pl.pallas_call(functools.partial(kernel, shards), out_shape=jax.ShapeDtyp...  50.8 us
    unnamed x1, local copies, waits for them, and re-layouts  1.59 us
    reshape x1, local copies, waits for them, and re-layouts, body(): norm_gain.reshape(1, width)  1.29 us

profile of v1, /device:TPU:0, one launch (start us, length us, event | category | flops | bytes accessed | tf_op | source)
XLA Modules:
  0.0 54.4 jit_solution(1116118221247363066)
XLA Ops:
  0.7 1.3 %reshape.10.gain = f32[1,1280]{1,0:T(1,128)} reshape(f32[1280]{0:T(1024)} %param.13) | data formatting | bytes 10240 | tf_op jit(solution)/shard_map/reshape | solution.py:232
  1.9 50.8 %shard_map.91 = bf16[64,1280]{1,0:T(8,128)(2,1)} custom-call(bf16[2,128,1280]{2,1,0:T(8,128)(2,1)} %bitcast.2, bf16[1280,1280]{1,0:T(8,128)(2,1)} %w_query.1, bf16[1280,2560]{1,0:T(8,128)(2,1)} %w_kv.1, bf16[1280,1280]{1,0:T(8,128)(2,1)} %w_out.1, f32[1,1280]{1,0:T(1,128)} %reshape.10.gain, s32[2,3]{1,0:T(2,128)} %owner.1, s32[2,3]{1,0:T(2,128)} %slot.1, ...), custom_call_target="tpu_custom_call" | custom-call | flops 20000000000 | bytes 20000000 | tf_op jit(solution)/shard_map/pallas_call | solution.py:207
  52.8 1.6 %copy.12 = bf16[64,1280]{1,0:T(8,128)(2,1)} copy(bf16[64,1280]{1,0:T(8,128)(2,1)} %shard_map.91) | data formatting | bytes 327680

commit v2 on v1

--- a/solution.py
+++ b/solution.py
@@ -10,14 +10,14 @@
 HEADS = 20
 BLOCK = 128
 POOL = 4
-TILE = 512
+TILE = 256
 MESH = pl.DeviceIdType.MESH
 F32 = jnp.float32
 BF16 = jnp.bfloat16
 
 
 def kernel(shards, frames, w_query, w_kv, w_out, gain, owner, slot, gpos, length, out,
-           fall, kv, wq_v, wkv_v, wout_v, q_v, gacc, gkv, pctx, proj, lsem, ssem, rsem, psem):
+           fall, kv, wq_v, wkv_v, wout_v, q_v, gacc, gkv, pctx, proj, s_a, s_b, m_a, m_b, lsem, ssem, rsem, kssem, krsem):
     me = lax.axis_index("tm")
     width = wq_v.shape[0]
     picks = owner.shape[1]
@@ -63,8 +63,6 @@
         send(frames.at[1], me, 1, near_y)
         send(frames.at[1], me, 1, near_x)
         send(frames.at[0], me, 0, near_y)
-        send(frames.at[0], me, 0, side)
-        send(frames.at[1], me, 1, side)
     else:
         for target in partners:
             send(frames.at[0], me, 0, target)
@@ -77,20 +75,62 @@
     def onehot(block):
         return jnp.where(pos_t == block * BLOCK + lane, 1.0, 0.0).astype(BF16)
 
+    passed = []
+
+    def pass_on(block, n):
+        part = kv.at[block, pl.ds(n * 2, 2)]
+        return pltpu.make_async_remote_copy(
+            src_ref=part, dst_ref=part, send_sem=kssem.at[block, n], recv_sem=krsem.at[block, n],
+            device_id={"tm": side}, device_id_type=MESH)
+
+    def add_global(n, hot, keys, vals_t):
+        far_k = jnp.dot(hot, keys, preferred_element_type=F32)
+        far_v = lax.dot_general(vals_t, hot, (((1,), (1,)), ((), ())), preferred_element_type=F32)
+        for j in range(2):
+            gacc[n * 2 + j, 0] += far_k[:, j * 128:(j + 1) * 128]
+            gacc[n * 2 + j, 1] += far_v[j * 128:(j + 1) * 128]
+
     def project(shard_a, part_a, shard_b, part_b):
         block_a, block_b = shard_a * 2 + part_a, shard_b * 2 + part_b
         hot = jnp.concatenate([onehot(block_a), onehot(block_b)], axis=1)
 
         def step(n, carry):
-            cols = pl.ds(pl.multiple_of(n * TILE, TILE), TILE)
+            kcols = pl.ds(pl.multiple_of(n * TILE, TILE), TILE)
+            vcols = pl.ds(pl.multiple_of(width + n * TILE, TILE), TILE)
             rows = jnp.concatenate([fall[shard_a, part_a], fall[shard_b, part_b]], axis=0)
-            made = jnp.dot(rows, wkv_v[:, cols], preferred_element_type=F32).astype(BF16)
-            kv[block_a, :, cols] = made[:BLOCK]
-            kv[block_b, :, cols] = made[BLOCK:]
-            gacc[:, cols] += jnp.dot(hot, made, preferred_element_type=F32)
+            keys = jnp.dot(rows, wkv_v[:, kcols], preferred_element_type=F32).astype(BF16)
+            vals_t = jnp.dot(rows, wkv_v[:, vcols], preferred_element_type=F32).T.astype(BF16)
+            for k, block in enumerate((block_a, block_b)):
+                for j in range(2):
+                    kv[block, n * 2 + j, 0] = keys[k * 128:(k + 1) * 128, j * 128:(j + 1) * 128]
+                    kv[block, n * 2 + j, 1] = vals_t[j * 128:(j + 1) * 128, k * 128:(k + 1) * 128]
+            if shards == 8:
+                pass_on(block_a, n).start()
+                pass_on(block_b, n).start()
+            add_global(n, hot, keys, vals_t)
             return carry
 
-        lax.fori_loop(0, 2 * width // TILE, step, 0)
+        lax.fori_loop(0, width // TILE, step, 0)
+        if shards == 8:
+            passed.append((block_a, block_b))
+
+    def take(shard_a, part_a, shard_b, part_b):
+        block_a, block_b = shard_a * 2 + part_a, shard_b * 2 + part_b
+        hot = jnp.concatenate([onehot(block_a), onehot(block_b)], axis=1)
+
+        def step(n, carry):
+            pass_on(block_a, n).wait_recv()
+            pass_on(block_b, n).wait_recv()
+            keys = jnp.concatenate([jnp.concatenate(
+                [kv[block, n * 2 + j, 0] for j in range(2)], axis=1)
+                for block in (block_a, block_b)], axis=0)
+            vals_t = jnp.concatenate([jnp.concatenate(
+                [kv[block, n * 2 + j, 1] for block in (block_a, block_b)], axis=1)
+                for j in range(2)], axis=0)
+            add_global(n, hot, keys, vals_t)
+            return carry
+
+        lax.fori_loop(0, width // TILE, step, 0)
 
     own.wait()
     got_q.wait()
@@ -109,35 +149,21 @@
         diag = near_x + near_y - me
         side_x, side_y = (v + 1 - 2 * (v % 2) for v in (near_x, near_y))
         side_d = diag + 1 - 2 * (diag % 2)
-        arrived(side, 0)
-        arrived(side, 1)
-        project(side, 0, side, 1)
         arrived(near_x, 0)
         send(fall.at[near_x, 0], near_x, 0, near_y)
-        send(fall.at[near_x, 0], near_x, 0, side)
         arrived(near_y, 1)
         send(fall.at[near_y, 1], near_y, 1, near_x)
-        send(fall.at[near_y, 1], near_y, 1, side)
         project(near_x, 0, near_y, 1)
-        arrived(side_x, 0)
-        arrived(side_y, 1)
-        project(side_x, 0, side_y, 1)
+        take(side, 0, side, 1)
+        take(side_x, 0, side_y, 1)
         arrived(near_x, 1)
-        send(fall.at[near_x, 1], near_x, 1, side)
         arrived(near_y, 0)
-        send(fall.at[near_y, 0], near_y, 0, side)
         project(near_x, 1, near_y, 0)
-        arrived(side_x, 1)
-        arrived(side_y, 0)
-        project(side_x, 1, side_y, 0)
+        take(side_x, 1, side_y, 0)
         arrived(diag, 0)
-        send(fall.at[diag, 0], diag, 0, side)
         arrived(diag, 1)
-        send(fall.at[diag, 1], diag, 1, side)
         project(diag, 0, diag, 1)
-        arrived(side_d, 0)
-        arrived(side_d, 1)
-        project(side_d, 0, side_d, 1)
+        take(side_d, 0, side_d, 1)
     else:
         for k in range(1, shards):
             source = (me + shards - k) % shards
@@ -152,33 +178,49 @@
     pool_row = lax.broadcasted_iota(jnp.int32, (BLOCK // POOL, BLOCK), 0)
     pool_col = lax.broadcasted_iota(jnp.int32, (BLOCK // POOL, BLOCK), 1)
     pool = jnp.where(pool_col // POOL == pool_row, 1.0 / POOL, 0.0).astype(BF16)
-    far_bias = jnp.where(gpos[...] < live * BLOCK, 0.0, -1e30)
+    far = jnp.where(pos_t >= live * BLOCK, -1e30, 0.0)
+    far = jnp.concatenate([far, far], axis=1)
     blocks, biases = [], []
     for b in range(2):
         ids = [first + b - 1 + k for k in range(3)]
         ids += [owner[b, j] * 2 + slot[b, j] for j in range(picks)]
         blocks.append([jnp.clip(i, 0, 2 * shards - 1) for i in ids])
-        row = [jnp.full((1, BLOCK), jnp.where((i >= 0) & (i < live), 0.0, -1e30), F32) for i in ids]
-        biases.append(jnp.concatenate(row + [far_bias], axis=1))
-
-    def pair_step(p, carry):
+        biases.append([jnp.where((i >= 0) & (i < live), 0.0, -1e30) for i in ids])
+
+    pairs = width // 128
+
+    def score(p, s_ref, m_ref):
         kcols = pl.ds(pl.multiple_of(p * 128, 128), 128)
-        vcols = pl.ds(pl.multiple_of(width + p * 128, 128), 128)
         for b in range(2):
             q = q_v[b * BLOCK:(b + 1) * BLOCK, kcols]
             qs = jnp.concatenate([q * low, q * high], axis=0)
-            keys = jnp.concatenate([kv[i, :, kcols] for i in blocks[b]] + [gkv[:, kcols]], axis=0)
-            vals = jnp.concatenate([kv[i, :, vcols] for i in blocks[b]] + [gkv[:, vcols]], axis=0)
-            s = lax.dot_general(qs, keys, (((1,), (1,)), ((), ())), preferred_element_type=F32)
-            s = s + biases[b]
-            e = jnp.exp(s - jnp.max(s, axis=1, keepdims=True))
-            total = jnp.sum(e, axis=1, keepdims=True)
-            o = jnp.dot(e.astype(BF16), vals, preferred_element_type=F32) / total
-            c = jnp.where(lane < 64, o[:BLOCK], o[BLOCK:]).astype(BF16)
-            pctx[b * 32:(b + 1) * 32, kcols] = jnp.dot(pool, c, preferred_element_type=F32)
+            keys = jnp.concatenate([kv[i, p, 0] for i in blocks[b]] + [gkv[p, 0]], axis=0)
+            s = lax.dot_general(keys, qs, (((1,), (1,)), ((), ())), preferred_element_type=F32)
+            near = [s[k * BLOCK:(k + 1) * BLOCK] + bias for k, bias in enumerate(biases[b])]
+            s = jnp.concatenate(near + [s[len(near) * BLOCK:] + far], axis=0)
+            s_ref[b] = s
+            m_ref[b] = jnp.max(s, axis=0, keepdims=True)
+
+    def combine(p, s_ref, m_ref):
+        kcols = pl.ds(pl.multiple_of(p * 128, 128), 128)
+        for b in range(2):
+            vals_t = jnp.concatenate([kv[i, p, 1] for i in blocks[b]] + [gkv[p, 1]], axis=1)
+            e = jnp.exp(s_ref[b] - m_ref[b])
+            scale = 1.0 / jnp.sum(e, axis=0, keepdims=True)
+            o = jnp.dot(vals_t, e.astype(BF16), preferred_element_type=F32) * scale
+            c = jnp.concatenate([o[:64, :BLOCK], o[64:, BLOCK:]], axis=0).astype(BF16)
+            pctx[b * 32:(b + 1) * 32, kcols] = lax.dot_general(
+                pool, c, (((1,), (1,)), ((), ())), preferred_element_type=F32)
+
+    def two_pairs(i, carry):
+        score(2 * i + 1, s_b, m_b)
+        combine(2 * i, s_a, m_a)
+        score(jnp.minimum(2 * i + 2, pairs - 1), s_a, m_a)
+        combine(2 * i + 1, s_b, m_b)
         return carry
 
-    lax.fori_loop(0, width // 128, pair_step, 0)
+    score(0, s_a, m_a)
+    lax.fori_loop(0, pairs // 2, two_pairs, 0)
     got_out.wait()
     rows = pctx.shape[0]
     upper = pctx[...].astype(BF16)
@@ -190,11 +232,18 @@
     pooled = proj[...]
     centered = pooled - jnp.mean(pooled, axis=1, keepdims=True)
     var = jnp.mean(centered * centered, axis=1, keepdims=True)
-    normed = centered * lax.rsqrt(var + 1e-05) * gain[...]
+    normed = centered * lax.rsqrt(var + 1e-05) * gain[...].reshape(1, width)
     row_block = first + lax.broadcasted_iota(jnp.int32, (rows, width), 0) * POOL // BLOCK
     out[...] = jnp.where(row_block < live, normed, 0.0).astype(BF16)
     for copy in sends:
         copy.wait_send()
+    for pair in passed:
+        for block in pair:
+            def sent(n, carry, block=block):
+                pass_on(block, n).wait_send()
+                return carry
+
+            lax.fori_loop(0, width // TILE, sent, 0)
 
 
 def body(shards, frames, w_query, w_kv, w_out, norm_gain, rand_owner, rand_slot, global_pos, length):
@@ -203,7 +252,8 @@
     hbm = pl.BlockSpec(memory_space=pl.ANY)
     vmem = pl.BlockSpec(memory_space=pltpu.VMEM)
     smem = pl.BlockSpec(memory_space=pltpu.SMEM)
-    n_sends = 14 if shards == 8 else 2 * (shards - 1)
+    keys = (4 + rand_owner.shape[1]) * BLOCK
+    n_sends = 6 if shards == 8 else 2 * (shards - 1)
     return pl.pallas_call(
         functools.partial(kernel, shards),
         out_shape=jax.ShapeDtypeStruct((local_rows // POOL, width), BF16),
@@ -211,25 +261,30 @@
         out_specs=vmem,
         scratch_shapes=[
             pltpu.VMEM((shards, 2, BLOCK, width), BF16),
-            pltpu.VMEM((2 * shards, BLOCK, 2 * width), BF16),
+            pltpu.VMEM((2 * shards, width // 128, 2, BLOCK, BLOCK), BF16),
             pltpu.VMEM((width, width), BF16),
             pltpu.VMEM((width, 2 * width), BF16),
             pltpu.VMEM((width, width), BF16),
             pltpu.VMEM((local_rows, width), BF16),
-            pltpu.VMEM((BLOCK, 2 * width), F32),
-            pltpu.VMEM((BLOCK, 2 * width), BF16),
+            pltpu.VMEM((width // 128, 2, BLOCK, BLOCK), F32),
+            pltpu.VMEM((width // 128, 2, BLOCK, BLOCK), BF16),
             pltpu.VMEM((local_rows // POOL, width), F32),
             pltpu.VMEM((local_rows // POOL, width), F32),
+            pltpu.VMEM((2, keys, 2 * BLOCK), F32),
+            pltpu.VMEM((2, keys, 2 * BLOCK), F32),
+            pltpu.VMEM((2, 1, 2 * BLOCK), F32),
+            pltpu.VMEM((2, 1, 2 * BLOCK), F32),
             pltpu.SemaphoreType.DMA((4,)),
             pltpu.SemaphoreType.DMA((n_sends,)),
             pltpu.SemaphoreType.DMA((shards, 2)),
-            pltpu.SemaphoreType.DMA((1,)),
+            pltpu.SemaphoreType.DMA((2 * shards, width // TILE)),
+            pltpu.SemaphoreType.DMA((2 * shards, width // TILE)),
         ],
         compiler_params=pltpu.CompilerParams(
             collective_id=0, has_side_effects=True, vmem_limit_bytes=60 * 1024 * 1024),
         cost_estimate=pl.CostEstimate(
             flops=20_000_000_000, bytes_accessed=20_000_000, transcendentals=5_000_000),
-    )(frames.reshape(2, BLOCK, width), w_query, w_kv, w_out, norm_gain.reshape(1, width),
+    )(frames.reshape(2, BLOCK, width), w_query, w_kv, w_out, norm_gain,
       rand_owner, rand_slot, global_pos.reshape(1, BLOCK), length)
 
 

time: 54.7 us -> 47.8 us (0.87)
  Pallas kernels: 50.8 us -> 45.2 us
  local copies, waits for them, and re-layouts: 2.89 us -> 1.59 us
    pallas_call x1, Pallas kernels: 50.8 us -> 45.2 us  [body(): pl.pallas_call(functools.partial(kernel, shards), out_shape=jax.ShapeDtyp...]
    reshape x1 -> x0, local copies, waits for them, and re-layouts: 1.29 us -> none  [body(): norm_gain.reshape(1, width)]
where the time goes in v2:
time: 47.8 us; the launch traced here: 47.5 us
  Pallas kernels  45.2 us (95%)
  local copies, waits for them, and re-layouts  1.59 us (3%)
  between operations  0.66 us (1%)
    pallas_call x1, Pallas kernels, body(): pl.pallas_call(functools.partial(kernel, shards), out_shape=jax.ShapeDtyp...  45.2 us
    unnamed x1, local copies, waits for them, and re-layouts  1.59 us

profile of v2, /device:TPU:0, one launch (start us, length us, event | category | flops | bytes accessed | tf_op | source)
XLA Modules:
  0.0 47.5 jit_solution(380644864094212434)
XLA Ops:
  0.7 45.2 %shard_map.91 = bf16[64,1280]{1,0:T(8,128)(2,1)} custom-call(bf16[2,128,1280]{2,1,0:T(8,128)(2,1)} %bitcast.2, bf16[1280,1280]{1,0:T(8,128)(2,1)} %w_query.1, bf16[1280,2560]{1,0:T(8,128)(2,1)} %w_kv.1, bf16[1280,1280]{1,0:T(8,128)(2,1)} %w_out.1, f32[1280]{0:T(1024)} %gain.1, s32[2,3]{1,0:T(2,128)} %owner.1, s32[2,3]{1,0:T(2,128)} %slot.1, ...), custom_call_target="tpu_custom_call" | custom-call | flops 20000000000 | bytes 20000000 | tf_op jit(solution)/shard_map/pallas_call | solution.py:257
  45.9 1.6 %copy.12 = bf16[64,1280]{1,0:T(8,128)(2,1)} copy(bf16[64,1280]{1,0:T(8,128)(2,1)} %shard_map.91) | data formatting | bytes 327680

commit v3 on v2

--- a/solution.py
+++ b/solution.py
@@ -110,7 +110,7 @@
             add_global(n, hot, keys, vals_t)
             return carry
 
-        lax.fori_loop(0, width // TILE, step, 0)
+        lax.fori_loop(0, width // TILE, step, 0, unroll=shards == 8)
         if shards == 8:
             passed.append((block_a, block_b))
 

time: 47.8 us -> 47.1 us (0.985)
  Pallas kernels: 45.2 us -> 44.6 us
    pallas_call x1, Pallas kernels: 45.2 us -> 44.6 us  [body(): pl.pallas_call(functools.partial(kernel, shards), out_shape=jax.ShapeDtyp...]
where the time goes in v3:
time: 47.1 us; the launch traced here: 46.8 us
  Pallas kernels  44.6 us (95%)
  local copies, waits for them, and re-layouts  1.59 us (3%)
  between operations  0.66 us (1%)
    pallas_call x1, Pallas kernels, body(): pl.pallas_call(functools.partial(kernel, shards), out_shape=jax.ShapeDtyp...  44.6 us
    unnamed x1, local copies, waits for them, and re-layouts  1.59 us

profile of v3, /device:TPU:0, one launch (start us, length us, event | category | flops | bytes accessed | tf_op | source)
XLA Modules:
  0.0 46.8 jit_solution(426076719771525267)
XLA Ops:
  0.7 44.6 %shard_map.91 = bf16[64,1280]{1,0:T(8,128)(2,1)} custom-call(bf16[2,128,1280]{2,1,0:T(8,128)(2,1)} %bitcast.2, bf16[1280,1280]{1,0:T(8,128)(2,1)} %w_query.1, bf16[1280,2560]{1,0:T(8,128)(2,1)} %w_kv.1, bf16[1280,1280]{1,0:T(8,128)(2,1)} %w_out.1, f32[1280]{0:T(1024)} %gain.1, s32[2,3]{1,0:T(2,128)} %owner.1, s32[2,3]{1,0:T(2,128)} %slot.1, ...), custom_call_target="tpu_custom_call" | custom-call | flops 20000000000 | bytes 20000000 | tf_op jit(solution)/shard_map/pallas_call | solution.py:257
  45.3 1.6 %copy.12 = bf16[64,1280]{1,0:T(8,128)(2,1)} copy(bf16[64,1280]{1,0:T(8,128)(2,1)} %shard_map.91) | data formatting | bytes 327680
